TPU v7x, 128 devices: a whole 4x4x4 slice. The times are simulated.
128 devices in a mesh: aud: 8 (over z, core), vid: 16 (over y, x).
Axes of the slice: x: 4, y: 4, z: 4, core: 2. Of those that a mesh axis runs over, the one named last changes fastest.
Arguments:
- audio: float32 [16384, 1024], P('aud', 'vid'), may hold values from -8 to 8
- video: float32 [16384, 1024], P('vid', 'aud'), may hold values from -8 to 8
- scale: float32 [], replicated, may hold values from 6 to 12
- bias: float32 [], replicated, may hold values from -7 to -5
Outputs:
- row_loss: float32 [16384], P('aud')
- grad_audio: float32 [16384, 1024], P('aud', 'vid')
- grad_video: float32 [16384, 1024], P('vid', 'aud')
All inputs are finite; a program needn't handle non-finite values.
Results may differ from a plain program's by a relative error of at most 0.0003.
Values sent between devices are 32-bit elements; how exact they have to be, the bound alone decides.
No kernel may reach another device: no remote copies, remote signals or barrier semaphores. Data moves between devices by JAX's collectives and lax.ppermute only.
A program may use at most 128 MiB of HBM per device.

v0:
```python
import jax
import jax.numpy as jnp
from jax import lax
from jax.experimental import pallas as pl
from jax.experimental.pallas import tpu as pltpu
from jax.sharding import Mesh, PartitionSpec as P

F32 = jnp.float32
BF16 = jnp.bfloat16
F8 = jnp.float8_e4m3fn
UP_VALUE = 2.0**8
UP_REST = 2.0**17
DOWN = 2.0**-25
EPS = 1e-06
CHUNKS = (1024, 1024)
BLOCK = 512
VMEM = 56 * 2**20
PLANE = ("core", "y", "x")
MIB = 2**20


def dot(a, b, dims):
    return lax.dot_general(a, b, (dims, ((), ())), preferred_element_type=F32)


def split(x, axis, value_first):
    high = x.astype(BF16)
    rest = ((x - high.astype(F32)) * UP_REST).astype(F8)
    value = (x * UP_VALUE).astype(F8)
    pair = (value, rest) if value_first else (rest, value)
    return high, jnp.concatenate(pair, axis=axis)


def product(a, b, dims):
    return dot(a[0], b[0], dims) + DOWN * dot(a[1], b[1], dims)


def prepare_kernel(place, own_ref, other_ref, inv_ref, unit_t_ref, v_high, v_small, t_high, t_small, whole, flipped):
    core, y, x, z = place[0], place[1], place[2], place[3]
    n = whole.shape[0]
    for k, ref in enumerate((own_ref, other_ref)):
        side = jnp.where(k == 0, core, 1 - core)
        for hops in range(4):
            at = 256 * lax.rem(z + 4 - hops, 4) + 128 * side
            whole[:, pl.ds(pl.multiple_of(at, 128), 128)] = ref[hops]
    v_t = whole[...].T
    inv = lax.rsqrt(jnp.sum(v_t * v_t, axis=0, keepdims=True) + EPS)
    inv_ref[...] = inv
    flipped[...] = (v_t * inv).reshape(16, 64, n)
    for outer in range(4):
        for inner in range(4):
            row = lax.rem(y + 4 - jnp.where(core == 0, outer, inner), 4)
            column = lax.rem(x + 4 - jnp.where(core == 0, inner, outer), 4)
            at = 64 * (4 * outer + inner)
            unit_t_ref[at : at + 64, :] = flipped[4 * row + column]
    unit_t = unit_t_ref[...]
    for (high, small), part, axis in (((t_high, t_small), unit_t, 1), ((v_high, v_small), unit_t.T, 1)):
        high[...], small[...] = split(part, axis, True)


def prepare(own, other, place):
    _, n, _ = own.shape
    whole = pl.BlockSpec(memory_space=pltpu.VMEM)
    shape = jax.ShapeDtypeStruct
    return pl.pallas_call(
        prepare_kernel,
        in_specs=[pl.BlockSpec(memory_space=pltpu.SMEM), whole, whole],
        out_specs=[whole] * 6,
        out_shape=[
            shape((1, n), F32),
            shape((1024, n), F32),
            shape((n, 1024), BF16),
            shape((n, 2048), F8),
            shape((1024, n), BF16),
            shape((1024, 2 * n), F8),
        ],
        scratch_shapes=[pltpu.VMEM((n, 1024), F32), pltpu.VMEM((16, 64, n), F32)],
        compiler_params=pltpu.CompilerParams(vmem_limit_bytes=VMEM),
        cost_estimate=pl.CostEstimate(flops=0, bytes_accessed=30 * MIB, transcendentals=0),
        name="video_parts",
    )(place, own, other)


def soft_tail(low):
    return jnp.where(low < 1e-3, low - 0.5 * low * low, jnp.log(1.0 + low))


def pairs_kernel(first, last, refs):
    place, scalars, *refs = refs
    audio, refs = refs[:4], refs[4:]
    _, unit_t_hbm, v_high, v_small, t_high, t_small, *refs = refs
    before = None
    if not first:
        before, *refs = refs
    grads_a, inv_ref, refs = refs[:4], refs[4], refs[5:]
    if last:
        mine, theirs, state, near, sem = refs
    else:
        state, near, sem = refs
    step = pl.program_id(0)
    scale, bias = scalars[0], scalars[1]
    n = v_high.shape[0]

    @pl.when(step == 0)
    def _():
        if first:
            state[...] = jnp.zeros_like(state)
        else:
            state[...] = before[...]

    audio_t = jnp.concatenate([r[...] for r in audio], axis=0)
    inv = lax.rsqrt(jnp.sum(audio_t * audio_t, axis=0, keepdims=True) + EPS)
    inv_ref[...] = inv
    unit_t = audio_t * inv
    block = unit_t.shape[1]
    scaled = scale * product((v_high[...], v_small[...]), split(unit_t, 0, False), ((1,), (0,)))
    logits = scaled + bias
    low = jnp.exp(-jnp.abs(logits))
    over = 1.0 / (1.0 + low)
    sig = jnp.where(logits >= 0, over, low * over)
    soft = jnp.maximum(logits, 0.0) + soft_tail(low)
    offset = place[3] + step * block
    paired = (
        lax.broadcasted_iota(jnp.int32, (n, block), 0)
        - lax.broadcasted_iota(jnp.int32, (n, block), 1)
    ) == offset
    away = jnp.where(paired, 0.0, sig)
    loss = jnp.sum(soft, axis=0, keepdims=True)
    grad_a = product((t_high[...], t_small[...]), split(away, 0, False), ((1,), (0,)))
    inner = jnp.sum(grad_a * unit_t, axis=0, keepdims=True)
    for k, ref in enumerate(grads_a):
        ref[0:256, :] = grad_a[256 * k : 256 * k + 256, :]
        ref[256:257, :] = loss
        ref[257:258, :] = inner
        ref[258:264, :] = jnp.zeros((6, block), F32)
    state[...] += product(split(unit_t, 1, True), split(away, 1, False), ((1,), (1,)))

    @pl.when((offset >= 0) & (offset < n))
    def _():
        at = pl.multiple_of(offset, block)
        copy = pltpu.make_async_copy(unit_t_hbm.at[:, pl.ds(at, block)], near, sem)
        copy.start()
        own = jnp.sum(jnp.where(paired, scaled, 0.0), axis=0, keepdims=True)
        value = own + bias
        low_own = jnp.exp(-jnp.abs(value))
        diag = jnp.where(value >= 0, 1.0, low_own) / (1.0 + low_own) - 1.0
        copy.wait()
        pull = near[...] * diag
        inner_own = jnp.sum(pull * unit_t, axis=0, keepdims=True)
        for k, ref in enumerate(grads_a):
            ref[0:256, :] += pull[256 * k : 256 * k + 256, :]
            ref[256:257, :] += -value
            ref[257:258, :] += inner_own
        state[:, pl.ds(at, block)] += unit_t * diag

    if last:

        @pl.when(step == pl.num_programs(0) - 1)
        def _():
            core, y, x, z = place[0], place[1], place[2], place[4]
            for half in range(n // block):
                lanes = pl.ds(half * block, block)
                copy = pltpu.make_async_copy(unit_t_hbm.at[:, lanes], near, sem)
                copy.start()
                copy.wait()
                row = jnp.sum(near[...] * state[:, lanes], axis=0, keepdims=True)
                for ref in (mine, theirs):
                    for owner in range(4):
                        ref[owner, 128:129, lanes] = row
            for k, ref in enumerate((mine, theirs)):
                side = jnp.where(k == 0, core, 1 - core)
                for owner in range(4):
                    ref[owner, 129:136, :] = jnp.zeros((7, n), F32)
                    dy = lax.rem(y + 8 - z - owner, 4)
                    for part in range(2):
                        dx = lax.rem(x + 4 - 2 * side - part, 4)
                        at = jnp.where(core == 0, 4 * dy + dx, 4 * dx + dy) * 64
                        rows = pl.ds(pl.multiple_of(at, 64), 64)
                        ref[owner, 64 * part : 64 * part + 64, :] = state[rows, :]


def pairs(audio, ahead, video, place, scalars, before, last):
    rows = audio[0].shape[1]
    first = before is None
    n = video[1].shape[0]
    smem = pl.BlockSpec(memory_space=pltpu.SMEM)
    still = lambda shape: pl.BlockSpec(shape, lambda i: (0, 0), pipeline_mode=pl.Buffered(1))
    moving = lambda height: pl.BlockSpec((height, BLOCK), lambda i: (0, i))
    shape = jax.ShapeDtypeStruct
    in_specs = [smem, smem] + [moving(256)] * 4 + [pl.BlockSpec(memory_space=pl.ANY)] * 2
    in_specs += [still(v.shape) for v in video[1:]]
    operands = [place, scalars, *audio, ahead, *video]
    out_specs = [moving(264)] * 4 + [moving(1)]
    out_shape = [shape((264, rows), F32)] * 4 + [shape((1, rows), F32)]
    scratch = [pltpu.VMEM((1024, BLOCK), F32), pltpu.SemaphoreType.DMA]
    aliases = {}
    if not first:
        if not last:
            aliases = {len(operands): 5}
        in_specs.append(still((1024, n)))
        operands.append(before)
    if last:
        out_specs += [pl.BlockSpec((4, 136, n), lambda i: (0, 0, 0), pipeline_mode=pl.Buffered(1))] * 2
        out_shape += [shape((4, 136, n), F32)] * 2
        scratch = [pltpu.VMEM((1024, n), F32)] + scratch
    else:
        out_specs.append(still((1024, n)))
        out_shape.append(shape((1024, n), F32))

    def body(*refs):
        pairs_kernel(first, last, refs)

    return pl.pallas_call(
        body,
        grid=(rows // BLOCK,),
        in_specs=in_specs,
        out_specs=out_specs,
        out_shape=out_shape,
        scratch_shapes=scratch,
        input_output_aliases=aliases,
        compiler_params=pltpu.CompilerParams(vmem_limit_bytes=VMEM),
        cost_estimate=pl.CostEstimate(
            flops=6 * 2 * rows * n * 1024, bytes_accessed=24 * MIB, transcendentals=3 * rows * n
        ),
        name="pairs_last" if last else "pairs_first" if first else "pairs_next",
    )(*operands)


def perm(inner, k):
    pairs_of = []
    for core in range(2):
        for y in range(4):
            for x in range(4):
                along_x = (core == 0) == inner
                to = (core, y, (x + k) % 4) if along_x else (core, (y + k) % 4, x)
                pairs_of.append((16 * core + 4 * y + x, 16 * to[0] + 4 * to[1] + to[2]))
    return pairs_of


def move(block, inner, k):
    return lax.ppermute(block, PLANE, perm(inner, k))


def hop(block, k):
    return lax.ppermute(block, "z", [(i, (i + k) % 4) for i in range(4)])


def together(*arrays):
    spec = pl.BlockSpec(memory_space=pl.ANY)
    return pl.pallas_call(
        lambda *refs: None,
        in_specs=[spec] * len(arrays),
        out_specs=[spec] * len(arrays),
        out_shape=[jax.ShapeDtypeStruct(a.shape, a.dtype) for a in arrays],
        input_output_aliases={i: i for i in range(len(arrays))},
        name="together",
    )(*arrays)


def swap(block):
    return lax.ppermute(block, "core", [(0, 1), (1, 0)])


def local(audio, video, scale, bias):
    z, core, y, x = (lax.axis_index(a) for a in ("z", "core", "y", "x"))
    n = video.shape[0]
    audio_t = audio.T
    piece, rows = audio_t.shape
    scalars = jnp.stack([scale, bias])
    base = (2 * z + core) * rows - (4 * y + x) * n

    up, down = hop(video, 1), hop(video, 3)
    row = [audio_t] + [move(audio_t, True, k) for k in (1, 2, 3)]
    gathered, starts, start = [], [], 0
    for part in CHUNKS:
        block = jnp.concatenate([r[:, start : start + part] for r in row], axis=0)
        if start == 0:
            up, down, block = together(up, down, block)
            far = jnp.concatenate([hop(up[: n // 2], 1), hop(down[n // 2 :], 3)], axis=0)
        gathered.append([block] + [move(block, False, k) for k in (1, 2, 3)])
        starts.append(start)
        start += part
    own = jnp.stack([video, up, far, down])
    other = swap(own)
    place = jnp.stack([core, y, x, z]).astype(jnp.int32)
    inv_v, *parts = prepare(own, other, place)
    state = None
    invs, halves = [], []
    for c, blocks in enumerate(gathered):
        at = jnp.stack([core, y, x, base + starts[c], z]).astype(jnp.int32)
        last = c == len(CHUNKS) - 1
        ahead = gathered[min(c + 1, len(CHUNKS) - 1)][0]
        outs = pairs(blocks, ahead, parts, at, scalars, state, last)
        grads, inv, state = outs[:4], outs[4], outs[5]
        invs.append(inv)
        if c > 0:
            *came, second, third, fourth, theirs = together(*came, *grads[1:4], outs[-1])
            halves.append(kept + came[0] + came[1] + came[2])
            grads = [grads[0], second, third, fourth]
        kept = grads[0]
        came = [move(grads[k], False, 4 - k) for k in (1, 2, 3)]
    halves.append(kept + came[0] + came[1] + came[2])
    half = outs[5] + swap(theirs)
    mid = n // 2
    below, above, halves[-1] = together(hop(half[2, :, :mid], 1), hop(half[2, :, mid:], 3), halves[-1])
    to_up = jnp.concatenate([half[1, :, :mid] + below, half[1, :, mid:]], axis=1)
    to_down = jnp.concatenate([half[3, :, :mid], half[3, :, mid:] + above], axis=1)
    total_v = half[0] + hop(to_up, 1) + hop(to_down, 3)
    to = [
        jnp.concatenate(
            [jnp.concatenate([h[64 * k : 64 * k + 64], h[256:264]], axis=0) for h in halves], axis=1
        )
        for k in range(4)
    ]
    total_a = to[0]
    for k in (1, 2, 3):
        total_a = total_a + move(to[k], True, 4 - k)
    inv_a = jnp.concatenate(invs, axis=1)
    row_loss, inner_a = total_a[64], total_a[65:66]
    grad_a = scale * (total_a[0:64] * inv_a - audio_t * (inv_a * inv_a * inner_a))
    grad_v = scale * (total_v[0:128] * inv_v - video.T * (inv_v * inv_v * total_v[128:129]))
    return row_loss, grad_a.T, grad_v.T


def solution(mesh):
    fine = Mesh(mesh.devices.reshape(4, 2, 4, 4), ("z", "core", "y", "x"))
    aud, vid = ("z", "core"), ("y", "x")
    return jax.shard_map(
        local,
        mesh=fine,
        in_specs=(P(aud, vid), P(vid, aud), P(), P()),
        out_specs=(P(aud), P(aud, vid), P(vid, aud)),
        check_vma=False,
    )
```

profile of v0, /device:TPU:0, one launch (start us, length us, event | category | flops | bytes accessed | tf_op | source)
XLA Modules:
  0.0 198.7 jit_solution(9535733939930891211)
XLA Ops:
  2.3 2.7 %collective-permute-start.3 = (f32[64,2048]{1,0:T(8,128)}, f32[64,2048]{1,0:T(8,128)S(1)}, u32[]{:S(2)}, u32[]{:S(2)}) collective-permute-start(f32[64,2048]{1,0:T(8,128)} %bitcast.53), channel_id=1, source_target_pairs={{0,2},{1,3},{2,0},{3,1},{4,6},{5,7},{6,4},{7,5},{8,10},{9,11},{10,... | collective-permute-start | bytes 1572872 | tf_op jit(solution)/shard_map/ppermute | solution.py:241
  8.4 2.1 %collective-permute-start.1 = (f32[1024,128]{1,0:T(8,128)}, f32[1024,128]{1,0:T(8,128)S(1)}, u32[]{:S(2)}, u32[]{:S(2)}) collective-permute-start(f32[1024,128]{1,0:T(8,128)} %param.5), channel_id=1, source_target_pairs={{0,96},{32,0},{64,32},{96,64},{1,97},{33,1},{65,33},{97,65},{2,98}... | collective-permute-start | bytes 1572872 | tf_op jit(solution)/shard_map/ppermute | solution.py:245
  12.3 5.7 %collective-permute-done.3 = f32[64,2048]{1,0:T(8,128)S(1)} collective-permute-done((f32[64,2048]{1,0:T(8,128)}, f32[64,2048]{1,0:T(8,128)S(1)}, u32[]{:S(2)}, u32[]{:S(2)}) %collective-permute-start.3) | collective-permute-done | bytes 524320 | tf_op jit(solution)/shard_map/ppermute | solution.py:241
  26.2 2.7 %collective-permute-start.9 = (f32[512,128]{1,0:T(8,128)S(1)}, f32[512,128]{1,0:T(8,128)S(1)}, u32[]{:S(2)}, u32[]{:S(2)}) collective-permute-start(f32[512,128]{1,0:T(8,128)S(1)} %slice.109), channel_id=1, source_target_pairs={{0,96},{32,0},{64,32},{96,64},{1,97},{33,1},{65,33},{97,65},{2,98}... | collective-permute-start | bytes 786440 | tf_op jit(solution)/shard_map/ppermute | solution.py:245
  29.0 4.1 %collective-permute-done.8 = f32[512,128]{1,0:T(8,128)S(1)} collective-permute-done((f32[512,128]{1,0:T(8,128)S(1)}, f32[512,128]{1,0:T(8,128)S(1)}, u32[]{:S(2)}, u32[]{:S(2)}) %collective-permute-start.8) | collective-permute-done | bytes 262176 | tf_op jit(solution)/shard_map/ppermute | solution.py:245
  35.9 2.9 %collective-permute-start.6 = (f32[256,1024]{1,0:T(8,128)S(1)}, f32[256,1024]{1,0:T(8,128)}, u32[]{:S(2)}, u32[]{:S(2)}) collective-permute-start(f32[256,1024]{1,0:T(8,128)S(1)} %copy-done.7), channel_id=1, source_target_pairs={{0,8},{1,9},{2,10},{3,11},{4,12},{5,13},{6,14},{7,15},{8,0},{9,1},... | collective-permute-start | bytes 3145736 | tf_op jit(solution)/shard_map/ppermute | solution.py:241
  46.7 10.7 %video_parts.1 = (f32[1,1024]{1,0:T(1,128)}, f32[1024,1024]{1,0:T(8,128)}, bf16[1024,1024]{1,0:T(8,128)(2,1)}, f8e4m3fn[1024,2048]{1,0:T(32,128)(4,1)}, bf16[102...) custom-call(s32[4]{0:T(128)} %pad_add_fusion.place, f32[4,1024,128]{2,1,0:T(8,128)} %copy-done.1, ...), custom_call_target="tpu_custom_call" | custom-call | bytes 31457280 | tf_op jit(solution)/shard_map/video_parts/pallas_call | solution.py:65
  57.4 2.7 %collective-permute-start.16 = (f32[256,1024]{1,0:T(8,128)S(1)}, f32[256,1024]{1,0:T(8,128)S(1)}, u32[]{:S(2)}, u32[]{:S(2)}) collective-permute-start(f32[256,1024]{1,0:T(8,128)S(1)} %pad_maximum_fusion.8.refs_6_.refs_2_), channel_id=1, source_target_pairs={{0,12},{1,13},{2,14},{3,15},{4,0},{5,1},{6,2},{7,3},{8,4},{9,5},{1... | collective-permute-start | bytes 3145736 | tf_op jit(solution)/shard_map/ppermute | solution.py:241
  60.1 2.9 %collective-permute-done.6.refs_4_ = f32[256,1024]{1,0:T(8,128)} collective-permute-done((f32[256,1024]{1,0:T(8,128)S(1)}, f32[256,1024]{1,0:T(8,128)}, u32[]{:S(2)}, u32[]{:S(2)}) %collective-permute-start.6) | collective-permute-done | bytes 1048608 | tf_op jit(solution)/shard_map/ppermute | solution.py:241
  63.5 30.4 %pairs_first.1 = (f32[264,1024]{1,0:T(8,128)}, f32[264,1024]{1,0:T(8,128)}, f32[264,1024]{1,0:T(8,128)}, f32[264,1024]{1,0:T(8,128)}, f32[1,1024]{1,0:T(1,128)}, /*index=5*/f32[1024,1024]{1,0:T(8,128)}) custom-call(s32[5]{0:T(128)} %stack.64.refs_0_, f32[2]{0:T(128)} %pad_maximum_fusion.12.refs_1_, f32[256,1024]{1,0:T(8,128)} %get-tuple-element.35.refs_2_, ...), custom_call_target="tpu_custom_call" | custom-call | flops 12884901888 | bytes 25165824 | tf_op jit(solution)/shard_map/pairs_first/pallas_call | solution.py:213
  94.2 2.2 %collective-permute-start.13 = (f32[264,1024]{1,0:T(8,128)}, f32[264,1024]{1,0:T(8,128)S(1)}, u32[]{:S(2)}, u32[]{:S(2)}) collective-permute-start(f32[264,1024]{1,0:T(8,128)} %get-tuple-element.46), channel_id=1, source_target_pairs={{0,4},{1,5},{2,6},{3,7},{4,8},{5,9},{6,10},{7,11},{8,12},{9,13},{1... | collective-permute-start | bytes 3244040 | tf_op jit(solution)/shard_map/ppermute | solution.py:241
  97.7 30.8 %pairs_last.1 = (f32[264,1024]{1,0:T(8,128)}, f32[264,1024]{1,0:T(8,128)}, f32[264,1024]{1,0:T(8,128)}, f32[264,1024]{1,0:T(8,128)}, f32[1,1024]{1,0:T(1,128)}, ...) custom-call(s32[5]{0:T(128)} %stack.75.refs_0_, f32[2]{0:T(128)} %pad_maximum_fusion.12.refs_1_, f32[256,1024]{1,0:T(8,128)} %copy-done.19, ...), custom_call_target="tpu_custom_call" | custom-call | flops 12884901888 | bytes 25165824 | tf_op jit(solution)/shard_map/pairs_last/pallas_call | solution.py:213
  130.3 2.1 %copy.20 = f32[1024,128]{0,1:T(8,128)} copy(f32[1024,128]{1,0:T(8,128)} %param.5) | data formatting | bytes 1048576 | tf_op args[1]
  132.4 2.7 %collective-permute-start.20 = (f32[264,1024]{1,0:T(8,128)}, f32[264,1024]{1,0:T(8,128)S(1)}, u32[]{:S(2)}, u32[]{:S(2)}) collective-permute-start(f32[264,1024]{1,0:T(8,128)} %get-tuple-element.58), channel_id=1, source_target_pairs={{0,12},{1,13},{2,14},{3,15},{4,0},{5,1},{6,2},{7,3},{8,4},{9,5},{1... | collective-permute-start | bytes 3244040 | tf_op jit(solution)/shard_map/ppermute | solution.py:241
  137.7 2.3 %add_add_fusion.1 = f32[264,1024]{1,0:T(8,128)S(1)} fusion(f32[264,1024]{1,0:T(8,128)} %get-tuple-element.54, f32[264,1024]{1,0:T(8,128)} %get-tuple-element.53, f32[264,1024]{1,0:T(8,128)} %get-tuple-element.43, f32[264,1024]{1,0:T(8,128)S(1)} %copy-done.4), kind=kLoop, calls=%fused_computation.2 | loop fusion | flops 811008 | bytes 5406720 | tf_op jit(solution)/shard_map/add | solution.py:298
  144.5 2.4 %collective-permute-start.18 = (f32[136,512]{1,0:T(8,128)S(1)}, f32[136,512]{1,0:T(8,128)S(1)}, u32[]{:S(2)}, u32[]{:S(2)}) collective-permute-start(f32[136,512]{1,0:T(8,128)S(1)} %get-tuple-element.75), channel_id=1, source_target_pairs={{0,32},{32,64},{64,96},{96,0},{1,33},{33,65},{65,97},{97,1},{2,34}... | collective-permute-start | bytes 835592 | tf_op jit(solution)/shard_map/ppermute | solution.py:245
  146.9 2.1 %collective-permute-start.19 = (f32[136,512]{1,0:T(8,128)S(1)}, f32[136,512]{1,0:T(8,128)S(1)}, u32[]{:S(2)}, u32[]{:S(2)}) collective-permute-start(f32[136,512]{1,0:T(8,128)S(1)} %get-tuple-element.74), channel_id=1, source_target_pairs={{0,96},{32,0},{64,32},{96,64},{1,97},{33,1},{65,33},{97,65},{2,98}... | collective-permute-start | bytes 835592 | tf_op jit(solution)/shard_map/ppermute | solution.py:245
  149.0 10.8 %collective-permute-done.20 = f32[264,1024]{1,0:T(8,128)S(1)} collective-permute-done((f32[264,1024]{1,0:T(8,128)}, f32[264,1024]{1,0:T(8,128)S(1)}, u32[]{:S(2)}, u32[]{:S(2)}) %collective-permute-start.20) | collective-permute-done | bytes 1081376 | tf_op jit(solution)/shard_map/ppermute | solution.py:241
  159.8 3.8 %collective-permute-done.22 = f32[264,1024]{1,0:T(8,128)S(1)} collective-permute-done((f32[264,1024]{1,0:T(8,128)}, f32[264,1024]{1,0:T(8,128)S(1)}, u32[]{:S(2)}, u32[]{:S(2)}) %collective-permute-start.22) | collective-permute-done | bytes 1081376 | tf_op jit(solution)/shard_map/ppermute | solution.py:241
  167.7 3.5 %collective-permute-start.26 = (f32[136,1024]{1,0:T(8,128)S(1)}, f32[136,1024]{1,0:T(8,128)S(1)}, u32[]{:S(2)}, u32[]{:S(2)}) collective-permute-start(f32[136,1024]{1,0:T(8,128)S(1)} %pad_maximum_fusion.10), channel_id=1, source_target_pairs={{0,32},{32,64},{64,96},{96,0},{1,33},{33,65},{65,97},{97,1},{2,34}... | collective-permute-start | bytes 1671176 | tf_op jit(solution)/shard_map/ppermute | solution.py:245
  174.4 3.4 %collective-permute-start.23 = (f32[72,2048]{1,0:T(8,128)}, f32[72,2048]{1,0:T(8,128)}, u32[]{:S(2)}, u32[]{:S(2)}) collective-permute-start(f32[72,2048]{1,0:T(8,128)} %get-tuple-element.92), channel_id=1, source_target_pairs={{0,3},{1,0},{2,1},{3,2},{4,7},{5,4},{6,5},{7,6},{8,11},{9,8},{10,9... | collective-permute-start | bytes 1769480 | tf_op jit(solution)/shard_map/ppermute | solution.py:241
  179.5 5.6 %collective-permute-done.26 = f32[136,1024]{1,0:T(8,128)S(1)} collective-permute-done((f32[136,1024]{1,0:T(8,128)S(1)}, f32[136,1024]{1,0:T(8,128)S(1)}, u32[]{:S(2)}, u32[]{:S(2)}) %collective-permute-start.26) | collective-permute-done | bytes 557088 | tf_op jit(solution)/shard_map/ppermute | solution.py:245
  186.4 5.4 %collective-permute-done.23 = f32[72,2048]{1,0:T(8,128)} collective-permute-done((f32[72,2048]{1,0:T(8,128)}, f32[72,2048]{1,0:T(8,128)}, u32[]{:S(2)}, u32[]{:S(2)}) %collective-permute-start.23) | collective-permute-done | bytes 589856 | tf_op jit(solution)/shard_map/ppermute | solution.py:241
  191.8 3.8 %collective-permute-done.25 = f32[72,2048]{1,0:T(8,128)} collective-permute-done((f32[72,2048]{1,0:T(8,128)}, f32[72,2048]{1,0:T(8,128)}, u32[]{:S(2)}, u32[]{:S(2)}) %collective-permute-start.25) | collective-permute-done | bytes 589856 | tf_op jit(solution)/shard_map/ppermute | solution.py:241
  (136 shorter events, 48.3 us)
Async XLA Ops:
  2.3 15.7 %collective-permute-start.3 = (f32[64,2048]{1,0:T(8,128)}, f32[64,2048]{1,0:T(8,128)S(1)}, u32[]{:S(2)}, u32[]{:S(2)}) collective-permute-start(f32[64,2048]{1,0:T(8,128)} %bitcast.53), channel_id=1, source_target_pairs={{0,2},{1,3},{2,0},{3,1},{4,6},{5,7},{6,4},{7,5},{8,10},{9,11},{10,... | collective-permute-start | bytes 1572872 | tf_op jit(solution)/shard_map/ppermute | solution.py:241
  5.0 13.8 %collective-permute-start.4 = (f32[64,2048]{1,0:T(8,128)}, f32[64,2048]{1,0:T(8,128)S(1)}, u32[]{:S(2)}, u32[]{:S(2)}) collective-permute-start(f32[64,2048]{1,0:T(8,128)} %bitcast.54), channel_id=1, source_target_pairs={{0,3},{1,0},{2,1},{3,2},{4,7},{5,4},{6,5},{7,6},{8,11},{9,8},{10,9... | collective-permute-start | bytes 1572872 | tf_op jit(solution)/shard_map/ppermute | solution.py:241
  6.4 15.5 %collective-permute-start = (f32[1024,128]{1,0:T(8,128)}, f32[1024,128]{1,0:T(8,128)S(1)}, u32[]{:S(2)}, u32[]{:S(2)}) collective-permute-start(f32[1024,128]{1,0:T(8,128)} %param.5), channel_id=1, source_target_pairs={{0,32},{32,64},{64,96},{96,0},{1,33},{33,65},{65,97},{97,1},{2,34}... | collective-permute-start | bytes 1572872 | tf_op jit(solution)/shard_map/ppermute | solution.py:245
  8.4 13.6 %collective-permute-start.1 = (f32[1024,128]{1,0:T(8,128)}, f32[1024,128]{1,0:T(8,128)S(1)}, u32[]{:S(2)}, u32[]{:S(2)}) collective-permute-start(f32[1024,128]{1,0:T(8,128)} %param.5), channel_id=1, source_target_pairs={{0,96},{32,0},{64,32},{96,64},{1,97},{33,1},{65,33},{97,65},{2,98}... | collective-permute-start | bytes 1572872 | tf_op jit(solution)/shard_map/ppermute | solution.py:245
  33.9 12.0 %collective-permute-start.10 = (f32[4,1024,128]{2,1,0:T(8,128)S(1)}, f32[4,1024,128]{2,1,0:T(8,128)}, u32[]{:S(2)}, u32[]{:S(2)}) collective-permute-start(f32[4,1024,128]{2,1,0:T(8,128)S(1)} %pad_maximum_fusion.own_ref), channel_id=1, source_target_pairs={{0,16},{16,0},{1,17},{17,1},{2,18},{18,2},{3,19},{19,3},{4,20},{20... | collective-permute-start | bytes 6291464 | tf_op jit(solution)/shard_map/ppermute | solution.py:261
  35.3 22.1 %collective-permute-start.5 = (f32[256,1024]{1,0:T(8,128)S(1)}, f32[256,1024]{1,0:T(8,128)}, u32[]{:S(2)}, u32[]{:S(2)}) collective-permute-start(f32[256,1024]{1,0:T(8,128)S(1)} %copy-done.7), channel_id=1, source_target_pairs={{0,4},{1,5},{2,6},{3,7},{4,8},{5,9},{6,10},{7,11},{8,12},{9,13},{1... | collective-permute-start | bytes 3145736 | tf_op jit(solution)/shard_map/ppermute | solution.py:241
  35.9 27.1 %collective-permute-start.6 = (f32[256,1024]{1,0:T(8,128)S(1)}, f32[256,1024]{1,0:T(8,128)}, u32[]{:S(2)}, u32[]{:S(2)}) collective-permute-start(f32[256,1024]{1,0:T(8,128)S(1)} %copy-done.7), channel_id=1, source_target_pairs={{0,8},{1,9},{2,10},{3,11},{4,12},{5,13},{6,14},{7,15},{8,0},{9,1},... | collective-permute-start | bytes 3145736 | tf_op jit(solution)/shard_map/ppermute | solution.py:241
  38.8 24.7 %collective-permute-start.7 = (f32[256,1024]{1,0:T(8,128)S(1)}, f32[256,1024]{1,0:T(8,128)}, u32[]{:S(2)}, u32[]{:S(2)}) collective-permute-start(f32[256,1024]{1,0:T(8,128)S(1)} %copy-done.7), channel_id=1, source_target_pairs={{0,12},{1,13},{2,14},{3,15},{4,0},{5,1},{6,2},{7,3},{8,4},{9,5},{1... | collective-permute-start | bytes 3145736 | tf_op jit(solution)/shard_map/ppermute | solution.py:241
  45.1 49.0 %collective-permute-start.14 = (f32[256,1024]{1,0:T(8,128)S(1)}, f32[256,1024]{1,0:T(8,128)S(1)}, u32[]{:S(2)}, u32[]{:S(2)}) collective-permute-start(f32[256,1024]{1,0:T(8,128)S(1)} %pad_maximum_fusion.8.refs_6_.refs_2_), channel_id=1, source_target_pairs={{0,4},{1,5},{2,6},{3,7},{4,8},{5,9},{6,10},{7,11},{8,12},{9,13},{1... | collective-permute-start | bytes 3145736 | tf_op jit(solution)/shard_map/ppermute | solution.py:241
  45.9 50.5 %collective-permute-start.15 = (f32[256,1024]{1,0:T(8,128)S(1)}, f32[256,1024]{1,0:T(8,128)S(1)}, u32[]{:S(2)}, u32[]{:S(2)}) collective-permute-start(f32[256,1024]{1,0:T(8,128)S(1)} %pad_maximum_fusion.8.refs_6_.refs_2_), channel_id=1, source_target_pairs={{0,8},{1,9},{2,10},{3,11},{4,12},{5,13},{6,14},{7,15},{8,0},{9,1},... | collective-permute-start | bytes 3145736 | tf_op jit(solution)/shard_map/ppermute | solution.py:241
  57.4 39.0 %collective-permute-start.16 = (f32[256,1024]{1,0:T(8,128)S(1)}, f32[256,1024]{1,0:T(8,128)S(1)}, u32[]{:S(2)}, u32[]{:S(2)}) collective-permute-start(f32[256,1024]{1,0:T(8,128)S(1)} %pad_maximum_fusion.8.refs_6_.refs_2_), channel_id=1, source_target_pairs={{0,12},{1,13},{2,14},{3,15},{4,0},{5,1},{6,2},{7,3},{8,4},{9,5},{1... | collective-permute-start | bytes 3145736 | tf_op jit(solution)/shard_map/ppermute | solution.py:241
  94.0 34.5 %collective-permute-start.11 = (f32[264,1024]{1,0:T(8,128)}, f32[264,1024]{1,0:T(8,128)S(1)}, u32[]{:S(2)}, u32[]{:S(2)}) collective-permute-start(f32[264,1024]{1,0:T(8,128)} %get-tuple-element.44), channel_id=1, source_target_pairs={{0,12},{1,13},{2,14},{3,15},{4,0},{5,1},{6,2},{7,3},{8,4},{9,5},{1... | collective-permute-start | bytes 3244040 | tf_op jit(solution)/shard_map/ppermute | solution.py:241
  94.1 34.4 %collective-permute-start.12 = (f32[264,1024]{1,0:T(8,128)}, f32[264,1024]{1,0:T(8,128)S(1)}, u32[]{:S(2)}, u32[]{:S(2)}) collective-permute-start(f32[264,1024]{1,0:T(8,128)} %get-tuple-element.45), channel_id=1, source_target_pairs={{0,8},{1,9},{2,10},{3,11},{4,12},{5,13},{6,14},{7,15},{8,0},{9,1},... | collective-permute-start | bytes 3244040 | tf_op jit(solution)/shard_map/ppermute | solution.py:241
  94.2 34.3 %collective-permute-start.13 = (f32[264,1024]{1,0:T(8,128)}, f32[264,1024]{1,0:T(8,128)S(1)}, u32[]{:S(2)}, u32[]{:S(2)}) collective-permute-start(f32[264,1024]{1,0:T(8,128)} %get-tuple-element.46), channel_id=1, source_target_pairs={{0,4},{1,5},{2,6},{3,7},{4,8},{5,9},{6,10},{7,11},{8,12},{9,13},{1... | collective-permute-start | bytes 3244040 | tf_op jit(solution)/shard_map/ppermute | solution.py:241
  132.4 27.3 %collective-permute-start.20 = (f32[264,1024]{1,0:T(8,128)}, f32[264,1024]{1,0:T(8,128)S(1)}, u32[]{:S(2)}, u32[]{:S(2)}) collective-permute-start(f32[264,1024]{1,0:T(8,128)} %get-tuple-element.58), channel_id=1, source_target_pairs={{0,12},{1,13},{2,14},{3,15},{4,0},{5,1},{6,2},{7,3},{8,4},{9,5},{1... | collective-permute-start | bytes 3244040 | tf_op jit(solution)/shard_map/ppermute | solution.py:241
  135.1 24.6 %collective-permute-start.21 = (f32[264,1024]{1,0:T(8,128)}, f32[264,1024]{1,0:T(8,128)S(1)}, u32[]{:S(2)}, u32[]{:S(2)}) collective-permute-start(f32[264,1024]{1,0:T(8,128)} %get-tuple-element.59), channel_id=1, source_target_pairs={{0,8},{1,9},{2,10},{3,11},{4,12},{5,13},{6,14},{7,15},{8,0},{9,1},... | collective-permute-start | bytes 3244040 | tf_op jit(solution)/shard_map/ppermute | solution.py:241
  136.3 27.3 %collective-permute-start.22 = (f32[264,1024]{1,0:T(8,128)}, f32[264,1024]{1,0:T(8,128)S(1)}, u32[]{:S(2)}, u32[]{:S(2)}) collective-permute-start(f32[264,1024]{1,0:T(8,128)} %get-tuple-element.60), channel_id=1, source_target_pairs={{0,4},{1,5},{2,6},{3,7},{4,8},{5,9},{6,10},{7,11},{8,12},{9,13},{1... | collective-permute-start | bytes 3244040 | tf_op jit(solution)/shard_map/ppermute | solution.py:241
  144.5 20.6 %collective-permute-start.18 = (f32[136,512]{1,0:T(8,128)S(1)}, f32[136,512]{1,0:T(8,128)S(1)}, u32[]{:S(2)}, u32[]{:S(2)}) collective-permute-start(f32[136,512]{1,0:T(8,128)S(1)} %get-tuple-element.75), channel_id=1, source_target_pairs={{0,32},{32,64},{64,96},{96,0},{1,33},{33,65},{65,97},{97,1},{2,34}... | collective-permute-start | bytes 835592 | tf_op jit(solution)/shard_map/ppermute | solution.py:245
  146.9 18.2 %collective-permute-start.19 = (f32[136,512]{1,0:T(8,128)S(1)}, f32[136,512]{1,0:T(8,128)S(1)}, u32[]{:S(2)}, u32[]{:S(2)}) collective-permute-start(f32[136,512]{1,0:T(8,128)S(1)} %get-tuple-element.74), channel_id=1, source_target_pairs={{0,96},{32,0},{64,32},{96,64},{1,97},{33,1},{65,33},{97,65},{2,98}... | collective-permute-start | bytes 835592 | tf_op jit(solution)/shard_map/ppermute | solution.py:245
  167.7 17.5 %collective-permute-start.26 = (f32[136,1024]{1,0:T(8,128)S(1)}, f32[136,1024]{1,0:T(8,128)S(1)}, u32[]{:S(2)}, u32[]{:S(2)}) collective-permute-start(f32[136,1024]{1,0:T(8,128)S(1)} %pad_maximum_fusion.10), channel_id=1, source_target_pairs={{0,32},{32,64},{64,96},{96,0},{1,33},{33,65},{65,97},{97,1},{2,34}... | collective-permute-start | bytes 1671176 | tf_op jit(solution)/shard_map/ppermute | solution.py:245
  171.2 13.9 %collective-permute-start.27 = (f32[136,1024]{1,0:T(8,128)S(1)}, f32[136,1024]{1,0:T(8,128)S(1)}, u32[]{:S(2)}, u32[]{:S(2)}) collective-permute-start(f32[136,1024]{1,0:T(8,128)S(1)} %pad_maximum_fusion.11), channel_id=1, source_target_pairs={{0,96},{32,0},{64,32},{96,64},{1,97},{33,1},{65,33},{97,65},{2,98}... | collective-permute-start | bytes 1671176 | tf_op jit(solution)/shard_map/ppermute | solution.py:245
  174.4 17.4 %collective-permute-start.23 = (f32[72,2048]{1,0:T(8,128)}, f32[72,2048]{1,0:T(8,128)}, u32[]{:S(2)}, u32[]{:S(2)}) collective-permute-start(f32[72,2048]{1,0:T(8,128)} %get-tuple-element.92), channel_id=1, source_target_pairs={{0,3},{1,0},{2,1},{3,2},{4,7},{5,4},{6,5},{7,6},{8,11},{9,8},{10,9... | collective-permute-start | bytes 1769480 | tf_op jit(solution)/shard_map/ppermute | solution.py:241
  177.8 14.0 %collective-permute-start.24 = (f32[72,2048]{1,0:T(8,128)S(1)}, f32[72,2048]{1,0:T(8,128)}, u32[]{:S(2)}, u32[]{:S(2)}) collective-permute-start(f32[72,2048]{1,0:T(8,128)S(1)} %get-tuple-element.93), channel_id=1, source_target_pairs={{0,2},{1,3},{2,0},{3,1},{4,6},{5,7},{6,4},{7,5},{8,10},{9,11},{10,... | collective-permute-start | bytes 1769480 | tf_op jit(solution)/shard_map/ppermute | solution.py:241
  179.2 16.4 %collective-permute-start.25 = (f32[72,2048]{1,0:T(8,128)}, f32[72,2048]{1,0:T(8,128)}, u32[]{:S(2)}, u32[]{:S(2)}) collective-permute-start(f32[72,2048]{1,0:T(8,128)} %pad_maximum_fusion.9), channel_id=1, source_target_pairs={{0,1},{1,2},{2,3},{3,0},{4,5},{5,6},{6,7},{7,4},{8,9},{9,10},{10,1... | collective-permute-start | bytes 1769480 | tf_op jit(solution)/shard_map/ppermute | solution.py:241
  (34 other events, 186.6 us)
where the time goes:
time: 199 us
  Pallas kernels  71.9 us (36%)
  waiting for transfers between devices  44.6 us (22%)
  starting transfers between devices  43.5 us (22%)
  local copies, waits for them, and re-layouts  20.5 us (10%)
  other arithmetic  15.8 us (8%)
  between operations  2.36 us (1%)
    pallas_call x2, Pallas kernels, pairs(): pl.pallas_call(body, grid=(rows // BLOCK,), in_specs=in_specs, out_specs=...  61.2 us
    ppermute x18, waiting for transfers between devices, move(): return lax.ppermute(block, PLANE, perm(inner, k))  32.9 us
    ppermute x18, starting transfers between devices, move(): return lax.ppermute(block, PLANE, perm(inner, k))  26.8 us
    ppermute x8, starting transfers between devices, hop(): return lax.ppermute(block, 'z', [(i, (i + k) % 4) for i in range(4)])  16.6 us
    unnamed x61, local copies, waits for them, and re-layouts  12.8 us
    ppermute x8, waiting for transfers between devices, hop(): return lax.ppermute(block, 'z', [(i, (i + k) % 4) for i in range(4)])  11.7 us
    pallas_call x1, Pallas kernels, prepare(): pl.pallas_call(prepare_kernel, in_specs=[pl.BlockSpec(memory_space=pltpu....  10.7 us
  transfers between devices with their start and end apart: 28, of which 11 were waited for; matrix products, arithmetic and copies ran while one was open for 11% of the time, Pallas kernels for 36%

commit v1 on v0

v1 whole, which is shorter than its diff:
```python
import jax
import jax.numpy as jnp
from jax import lax
from jax.experimental import pallas as pl
from jax.experimental.pallas import tpu as pltpu
from jax.sharding import Mesh, PartitionSpec as P

F32 = jnp.float32
BF16 = jnp.bfloat16
F8 = jnp.float8_e4m3fn
UP_VALUE = 2.0**8
UP_REST = 2.0**17
DOWN = 2.0**-25
EPS = 1e-06
CHUNKS = (1024, 1024)
BLOCK = 512
SUBS = 2
VMEM = 56 * 2**20
PLANE = ("core", "y", "x")
MIB = 2**20


def dot(a, b, dims):
    return lax.dot_general(a, b, (dims, ((), ())), preferred_element_type=F32)


def split(x, axis, value_first):
    high = x.astype(BF16)
    rest = ((x - high.astype(F32)) * UP_REST).astype(F8)
    value = (x * UP_VALUE).astype(F8)
    pair = (value, rest) if value_first else (rest, value)
    return high, jnp.concatenate(pair, axis=axis)


def product(a, b, dims):
    return dot(a[0], b[0], dims) + DOWN * dot(a[1], b[1], dims)


def prepare_kernel(place, whole, inv_ref, unit_t_ref, v_high, v_small, t_high, t_small, flipped):
    core, y, x = place[0], place[1], place[2]
    n = whole.shape[0]
    v_t = whole[...].T
    inv = lax.rsqrt(jnp.sum(v_t * v_t, axis=0, keepdims=True) + EPS)
    inv_ref[...] = inv
    flipped[...] = (v_t * inv).reshape(16, 64, n)
    for outer in range(4):
        for inner in range(4):
            row = lax.rem(y + 4 - jnp.where(core == 0, outer, inner), 4)
            column = lax.rem(x + 4 - jnp.where(core == 0, inner, outer), 4)
            at = 64 * (4 * outer + inner)
            unit_t_ref[at : at + 64, :] = flipped[4 * row + column]
    unit_t = unit_t_ref[...]
    for (high, small), part, axis in (((t_high, t_small), unit_t, 1), ((v_high, v_small), unit_t.T, 1)):
        high[...], small[...] = split(part, axis, True)


def prepare(video, place):
    n = video.shape[0]
    whole = pl.BlockSpec(memory_space=pltpu.VMEM)
    shape = jax.ShapeDtypeStruct
    return pl.pallas_call(
        prepare_kernel,
        in_specs=[pl.BlockSpec(memory_space=pltpu.SMEM), whole],
        out_specs=[whole] * 6,
        out_shape=[
            shape((1, n), F32),
            shape((1024, n), F32),
            shape((n, 1024), BF16),
            shape((n, 2048), F8),
            shape((1024, n), BF16),
            shape((1024, 2 * n), F8),
        ],
        scratch_shapes=[pltpu.VMEM((16, 64, n), F32)],
        compiler_params=pltpu.CompilerParams(vmem_limit_bytes=VMEM),
        cost_estimate=pl.CostEstimate(flops=0, bytes_accessed=16 * MIB, transcendentals=0),
        name="video_parts",
    )(place, video)


def inverse(d):
    r = pl.reciprocal(d, approx=True)
    return r * (2.0 - d * r)


def soft(power):
    return jnp.where(power < 1e-3, power - 0.5 * power * power, jnp.log(1.0 + power))


def pairs_kernel(first, last, refs):
    place, scalars, *refs = refs
    audio, refs = refs[:4], refs[4:]
    _, unit_t_hbm, *sources = refs[:6]
    refs = refs[6:]
    before = None
    if not first:
        before, *refs = refs
    grads_a, inv_ref, refs = refs[:4], refs[4], refs[5:]
    if last:
        whole, *refs = refs
    state, near, v_high, v_small, t_high, t_small, sem, sems = refs
    step = pl.program_id(0)
    scale, bias = scalars[0], scalars[1]
    n = v_high.shape[0]
    block = inv_ref.shape[1]
    sub = block // SUBS
    offset = place[3] + step * block
    loads = [
        pltpu.make_async_copy(source, to, sems.at[k])
        for k, (source, to) in enumerate(zip(sources, (v_high, v_small, t_high, t_small)))
    ]
    if not first:
        loads.append(pltpu.make_async_copy(before, state, sems.at[4]))

    @pl.when(step == 0)
    def _():
        for load in loads:
            load.start()
        if first:
            state[...] = jnp.zeros_like(state)

    audio_t = jnp.concatenate([r[...] for r in audio], axis=0)
    inv = lax.rsqrt(jnp.sum(audio_t * audio_t, axis=0, keepdims=True) + EPS)
    inv_ref[...] = inv
    unit_t = audio_t * inv

    @pl.when(step == 0)
    def _():
        for load in loads[:2]:
            load.wait()

    def similar(k):
        part = split(unit_t[:, k * sub : (k + 1) * sub], 0, False)
        return scale * product((v_high[...], v_small[...]), part, ((1,), (0,)))

    def judge(k, scaled):
        power = jnp.exp(scaled + bias)
        sig = power * inverse(1.0 + power)
        paired = (
            lax.broadcasted_iota(jnp.int32, (n, sub), 0)
            - lax.broadcasted_iota(jnp.int32, (n, sub), 1)
        ) == offset + k * sub
        loss = jnp.sum(soft(power), axis=0, keepdims=True)
        return paired, split(jnp.where(paired, 0.0, sig), 0, False), loss

    def pull_rows(k, away, loss):
        lanes = slice(k * sub, (k + 1) * sub)
        grad_a = product((t_high[...], t_small[...]), away, ((1,), (0,)))
        inner = jnp.sum(grad_a * unit_t[:, lanes], axis=0, keepdims=True)
        for p, ref in enumerate(grads_a):
            ref[0:256, lanes] = grad_a[256 * p : 256 * p + 256, :]
            ref[256:257, lanes] = loss
            ref[257:258, lanes] = inner
            ref[258:264, lanes] = jnp.zeros((6, sub), F32)

    scores = [similar(k) for k in range(SUBS)]
    judged = [judge(0, scores[0])]

    @pl.when(step == 0)
    def _():
        for load in loads[2:]:
            load.wait()

    for k in range(SUBS):
        if k > 0:
            judged.append(judge(k, scores[k]))
        pull_rows(k, judged[k][1], judged[k][2])
    high = jnp.concatenate([j[1][0] for j in judged], axis=1)
    small = jnp.concatenate([j[1][1][:n] for j in judged] + [j[1][1][n:] for j in judged], axis=1)
    state[...] += product(split(unit_t, 1, True), (high, small), ((1,), (1,)))

    @pl.when((offset >= 0) & (offset < n))
    def _():
        at = pl.multiple_of(offset, block)
        copy = pltpu.make_async_copy(unit_t_hbm.at[:, pl.ds(at, block)], near, sem)
        copy.start()
        own = jnp.concatenate(
            [jnp.sum(jnp.where(j[0], s, 0.0), axis=0, keepdims=True) for j, s in zip(judged, scores)],
            axis=1,
        )
        value = own + bias
        diag = -1.0 / (1.0 + jnp.exp(value))
        copy.wait()
        pull = near[...] * diag
        inner_own = jnp.sum(pull * unit_t, axis=0, keepdims=True)
        for k, ref in enumerate(grads_a):
            ref[0:256, :] += pull[256 * k : 256 * k + 256, :]
            ref[256:257, :] += -value
            ref[257:258, :] += inner_own
        state[:, pl.ds(at, block)] += unit_t * diag

    if last:

        @pl.when(step == pl.num_programs(0) - 1)
        def _():
            core, y, x = place[0], place[1], place[2]
            for half in range(n // block):
                lanes = pl.ds(half * block, block)
                copy = pltpu.make_async_copy(unit_t_hbm.at[:, lanes], near, sem)
                copy.start()
                copy.wait()
                row = jnp.sum(near[...] * state[:, lanes], axis=0, keepdims=True)
                for owner in range(8):
                    whole[owner, 128:129, lanes] = row
            for owner in range(8):
                whole[owner, 129:136, :] = jnp.zeros((7, n), F32)
                for part in range(2):
                    dy = lax.rem(y + 4 - owner // 2, 4)
                    dx = lax.rem(x + 4 - 2 * (owner % 2) - part, 4)
                    at = jnp.where(core == 0, 4 * dy + dx, 4 * dx + dy) * 64
                    rows = pl.ds(pl.multiple_of(at, 64), 64)
                    whole[owner, 64 * part : 64 * part + 64, :] = state[rows, :]


def pairs(audio, ahead, video, place, scalars, before, last):
    rows = audio[0].shape[1]
    first = before is None
    n = video[1].shape[0]
    smem = pl.BlockSpec(memory_space=pltpu.SMEM)
    still = lambda shape: pl.BlockSpec(shape, lambda i: (0, 0), pipeline_mode=pl.Buffered(1))
    moving = lambda height: pl.BlockSpec((height, BLOCK), lambda i: (0, i))
    shape = jax.ShapeDtypeStruct
    anywhere = pl.BlockSpec(memory_space=pl.ANY)
    in_specs = [smem, smem] + [moving(256)] * 4 + [anywhere] * 6
    operands = [place, scalars, *audio, ahead, *video]
    out_specs = [moving(264)] * 4 + [moving(1)]
    out_shape = [shape((264, rows), F32)] * 4 + [shape((1, rows), F32)]
    scratch = [pltpu.VMEM((1024, BLOCK), F32)] + [pltpu.VMEM(v.shape, v.dtype) for v in video[1:]]
    scratch += [pltpu.SemaphoreType.DMA, pltpu.SemaphoreType.DMA((5,))]
    if not first:
        in_specs.append(anywhere)
        operands.append(before)
    if last:
        out_specs.append(pl.BlockSpec((8, 136, n), lambda i: (0, 0, 0), pipeline_mode=pl.Buffered(1)))
        out_shape.append(shape((8, 136, n), F32))
        scratch = [pltpu.VMEM((1024, n), F32)] + scratch
    else:
        out_specs.append(still((1024, n)))
        out_shape.append(shape((1024, n), F32))

    def body(*refs):
        pairs_kernel(first, last, refs)

    return pl.pallas_call(
        body,
        grid=(rows // BLOCK,),
        in_specs=in_specs,
        out_specs=out_specs,
        out_shape=out_shape,
        scratch_shapes=scratch,
        compiler_params=pltpu.CompilerParams(vmem_limit_bytes=VMEM),
        cost_estimate=pl.CostEstimate(
            flops=6 * 2 * rows * n * 1024, bytes_accessed=24 * MIB, transcendentals=3 * rows * n
        ),
        name="pairs_last" if last else "pairs_first" if first else "pairs_next",
    )(*operands)


def perm(inner, k):
    pairs_of = []
    for core in range(2):
        for y in range(4):
            for x in range(4):
                along_x = (core == 0) == inner
                to = (core, y, (x + k) % 4) if along_x else (core, (y + k) % 4, x)
                pairs_of.append((16 * core + 4 * y + x, 16 * to[0] + 4 * to[1] + to[2]))
    return pairs_of


def move(block, inner, k):
    return lax.ppermute(block, PLANE, perm(inner, k))


def after(arrays, late):
    spec = pl.BlockSpec(memory_space=pl.ANY)
    return pl.pallas_call(
        lambda *refs: None,
        in_specs=[spec] * (len(arrays) + len(late)),
        out_specs=[spec] * len(late),
        out_shape=[jax.ShapeDtypeStruct(a.shape, a.dtype) for a in late],
        input_output_aliases={len(arrays) + i: i for i in range(len(late))},
        name="after",
    )(*arrays, *late)


def local(audio, video, scale, bias):
    z, core, y, x = (lax.axis_index(a) for a in ("z", "core", "y", "x"))
    n = video.shape[0]
    audio_t = audio.T
    rows = audio_t.shape[1]
    scalars = jnp.stack([scale, bias])
    base = (2 * z + core) * rows - (4 * y + x) * n

    whole_video = lax.all_gather(video, ("z", "core"), axis=1, tiled=True)
    row = [audio_t] + [move(audio_t, True, k) for k in (1, 2, 3)]
    gathered, starts, start = [], [], 0
    for part in CHUNKS:
        block = jnp.concatenate([r[:, start : start + part] for r in row], axis=0)
        gathered.append([block] + [move(block, False, k) for k in (1, 2, 3)])
        starts.append(start)
        start += part
    place = jnp.stack([core, y, x]).astype(jnp.int32)
    inv_v, *parts = prepare(whole_video, place)
    state = None
    invs, halves = [], []
    for c, blocks in enumerate(gathered):
        at = jnp.stack([core, y, x, base + starts[c]]).astype(jnp.int32)
        last = c == len(CHUNKS) - 1
        ahead = gathered[min(c + 1, len(CHUNKS) - 1)][0]
        outs = pairs(blocks, ahead, parts, at, scalars, state, last)
        grads, inv, state = outs[:4], outs[4], outs[5]
        invs.append(inv)
        if c > 0:
            seen = came[0][256:264] + came[1][256:264] + came[2][256:264]
            *others, state = after([seen], [*grads[1:], state])
            grads = [grads[0], *others]
            halves.append(kept + came[0] + came[1] + came[2])
        kept = grads[0]
        came = [move(grads[k], False, 4 - k) for k in (1, 2, 3)]
    halves.append(kept + came[0] + came[1] + came[2])

    total_v = lax.psum_scatter(state.reshape(1088, n), ("z", "core"), scatter_dimension=0, tiled=True)
    to = [
        jnp.concatenate(
            [jnp.concatenate([h[64 * k : 64 * k + 64], h[256:264]], axis=0) for h in halves], axis=1
        )
        for k in range(4)
    ]
    total_a = to[0]
    for k in (1, 2, 3):
        total_a = total_a + move(to[k], True, 4 - k)
    inv_a = jnp.concatenate(invs, axis=1)
    row_loss, inner_a = total_a[64], total_a[65:66]
    grad_a = scale * (total_a[0:64] * inv_a - audio_t * (inv_a * inv_a * inner_a))
    grad_v = scale * (total_v[0:128] * inv_v - video.T * (inv_v * inv_v * total_v[128:129]))
    return row_loss, grad_a.T, grad_v.T


def solution(mesh):
    fine = Mesh(mesh.devices.reshape(4, 2, 4, 4), ("z", "core", "y", "x"))
    aud, vid = ("z", "core"), ("y", "x")
    return jax.shard_map(
        local,
        mesh=fine,
        in_specs=(P(aud, vid), P(vid, aud), P(), P()),
        out_specs=(P(aud), P(aud, vid), P(vid, aud)),
        check_vma=False,
    )
```

time: 199 us -> 191 us (0.960); the launches traced: 199 us -> 188 us
  local copies, waits for them, and re-layouts: 20.5 us -> 5.36 us
  waiting for transfers between devices: 44.6 us -> 58.4 us
  between operations: 2.36 us -> 15.6 us
  starting transfers between devices: 43.5 us -> 30.8 us
  Pallas kernels: 71.9 us -> 66.2 us
  other arithmetic: 15.8 us -> 11.4 us
    ppermute x10 -> x0, starting transfers between devices: 16.7 us -> none  [the longest x8 16.6 us: hop(): return lax.ppermute(block, 'z', [(i, (i + k) % 4) for i in range(4)])]
    ppermute x18, waiting for transfers between devices: 32.9 us -> 48.5 us  [move(): return lax.ppermute(block, PLANE, perm(inner, k))]
    ppermute x10 -> x0, waiting for transfers between devices: 11.7 us -> none  [the longest x8 11.7 us: hop(): return lax.ppermute(block, 'z', [(i, (i + k) % 4) for i in range(4)])]
    all_gather x0 -> x1, waiting for transfers between devices: none -> 9.15 us  [local(): whole_video = lax.all_gather(video, ('z', 'core'), axis=1, tiled=True)]
    unnamed x61 -> x25, local copies, waits for them, and re-layouts: 12.8 us -> 4.05 us
    pallas_call x2, Pallas kernels: 61.2 us -> 56.2 us  [pairs(): pl.pallas_call(body, grid=(rows // BLOCK,), in_specs=in_specs, out_specs=...]
    ppermute x18, starting transfers between devices: 26.8 us -> 30.7 us  [move(): return lax.ppermute(block, PLANE, perm(inner, k))]
    add x3 -> x1, other arithmetic: 3.28 us -> 0.62 us  [local(): seen = came[0][256:264] + came[1][256:264] + came[2][256:264]]
  transfers between devices with their start and end apart: 28 -> 20, of which waited for: 11 -> 8; matrix products, arithmetic and copies ran while one was open for 11% -> 6% of each run, Pallas kernels for 36% -> 35%
where the time goes in v1:
time: 191 us; the launch traced here: 188 us
  Pallas kernels  66.2 us (35%)
  waiting for transfers between devices  58.4 us (31%)
  starting transfers between devices  30.8 us (16%)
  between operations  15.6 us (8%)
  other arithmetic  11.4 us (6%)
  local copies, waits for them, and re-layouts  5.36 us (3%)
    pallas_call x2, Pallas kernels, pairs(): pl.pallas_call(body, grid=(rows // BLOCK,), in_specs=in_specs, out_specs=...  56.2 us
    ppermute x18, waiting for transfers between devices, move(): return lax.ppermute(block, PLANE, perm(inner, k))  48.5 us
    ppermute x18, starting transfers between devices, move(): return lax.ppermute(block, PLANE, perm(inner, k))  30.7 us
    pallas_call x1, Pallas kernels, prepare(): pl.pallas_call(prepare_kernel, in_specs=[pl.BlockSpec(memory_space=pltpu....  10 us
    all_gather x1, waiting for transfers between devices, local(): whole_video = lax.all_gather(video, ('z', 'core'), axis=1, tiled=True)  9.15 us
    unnamed x25, local copies, waits for them, and re-layouts  4.05 us
  transfers between devices with their start and end apart: 20, of which 8 were waited for; matrix products, arithmetic and copies ran while one was open for 6% of the time, Pallas kernels for 35%

profile of v1, /device:TPU:0, one launch (start us, length us, event | category | flops | bytes accessed | tf_op | source)
XLA Modules:
  0.0 187.6 jit_solution(11368729679458236678)
XLA Ops:
  7.9 1.6 collective-permute-start
  9.6 2.7 %collective-permute-start.1 = (f32[64,2048]{1,0:T(8,128)}, f32[64,2048]{1,0:T(8,128)S(1)}, u32[]{:S(2)}, u32[]{:S(2)}) collective-permute-start(f32[64,2048]{1,0:T(8,128)} %bitcast.25), channel_id=1, source_target_pairs={{0,2},{1,3},{2,0},{3,1},{4,6},{5,7},{6,4},{7,5},{8,10},{9,11},{10,... | collective-permute-start | bytes 1572872 | tf_op jit(solution)/shard_map/ppermute | solution.py:270
  12.3 1.4 collective-permute-start.2
  14.8 3.8 %collective-permute-done = f32[64,2048]{1,0:T(8,128)S(1)} collective-permute-done((f32[64,2048]{1,0:T(8,128)}, f32[64,2048]{1,0:T(8,128)S(1)}, u32[]{:S(2)}, u32[]{:S(2)}) %collective-permute-start) | collective-permute-done | bytes 524320 | tf_op jit(solution)/shard_map/ppermute | solution.py:270
  18.7 6.6 %collective-permute-done.1 = f32[64,2048]{1,0:T(8,128)S(1)} collective-permute-done((f32[64,2048]{1,0:T(8,128)}, f32[64,2048]{1,0:T(8,128)S(1)}, u32[]{:S(2)}, u32[]{:S(2)}) %collective-permute-start.1) | collective-permute-done | bytes 524320 | tf_op jit(solution)/shard_map/ppermute | solution.py:270
  25.5 1.6 collective-permute-start.3
  27.1 2.9 %collective-permute-start.4 = (f32[256,1024]{1,0:T(8,128)S(1)}, f32[256,1024]{1,0:T(8,128)}, u32[]{:S(2)}, u32[]{:S(2)}) collective-permute-start(f32[256,1024]{1,0:T(8,128)S(1)} %pad_maximum_fusion.6.refs_2_), channel_id=1, source_target_pairs={{0,8},{1,9},{2,10},{3,11},{4,12},{5,13},{6,14},{7,15},{8,0},{9,1},... | collective-permute-start | bytes 3145736 | tf_op jit(solution)/shard_map/ppermute | solution.py:270
  36.4 3.0 %collective-permute-start.11 = (f32[256,1024]{1,0:T(8,128)}, f32[256,1024]{1,0:T(8,128)}, u32[]{:S(2)}, u32[]{:S(2)}) collective-permute-start(f32[256,1024]{1,0:T(8,128)} %pad_maximum_fusion.7.refs_6_.refs_2_), channel_id=1, source_target_pairs={{0,12},{1,13},{2,14},{3,15},{4,0},{5,1},{6,2},{7,3},{8,4},{9,5},{1... | collective-permute-start | bytes 3145736 | tf_op jit(solution)/shard_map/ppermute | solution.py:270
  39.4 9.2 %all-gather.2.cloned.1.call-done.whole = f32[1024,1024]{1,0:T(8,128)} async-done(((f32[1024,128]{1,0:T(8,128)}), f32[1024,1024]{1,0:T(8,128)}) %all-gather.2.cloned.1.call-update) | async-done | bytes 4194320 | tf_op jit(solution)/shard_map/all_gather | solution.py:293
  48.6 10.0 %video_parts.1 = (f32[1,1024]{1,0:T(1,128)}, f32[1024,1024]{1,0:T(8,128)}, bf16[1024,1024]{1,0:T(8,128)(2,1)}, f8e4m3fn[1024,2048]{1,0:T(32,128)(4,1)}, bf16[102...) custom-call(s32[3]{0:T(128)} %pad_add_fusion.2.place, f32[1024,1024]{1,0:T(8,128)} %all-gather.2.cloned.1.call-done.whole), custom_call_target="tpu_custom_call" | custom-call | bytes 16777216 | tf_op jit(solution)/shard_map/video_parts/pallas_call | solution.py:61
  58.6 1.7 collective-permute-start.9
  60.3 28.6 %pairs_first.1 = (f32[264,1024]{1,0:T(8,128)}, f32[264,1024]{1,0:T(8,128)}, f32[264,1024]{1,0:T(8,128)}, f32[264,1024]{1,0:T(8,128)}, f32[1,1024]{1,0:T(1,128)}, /*index=5*/f32[1024,1024]{1,0:T(8,128)}) custom-call(s32[4]{0:T(128)} %pad_add_fusion.refs_0_, f32[2]{0:T(128)} %pad_maximum_fusion.9.refs_1_, f32[256,1024]{1,0:T(8,128)} %copy-done.5, ...), custom_call_target="tpu_custom_call" | custom-call | flops 12884901888 | bytes 25165824 | tf_op jit(solution)/shard_map/pairs_first/pallas_call | solution.py:243
  89.0 2.9 %collective-permute-start.7 = (f32[264,1024]{1,0:T(8,128)}, f32[264,1024]{1,0:T(8,128)S(1)}, u32[]{:S(2)}, u32[]{:S(2)}) collective-permute-start(f32[264,1024]{1,0:T(8,128)} %get-tuple-element.32), channel_id=1, source_target_pairs={{0,8},{1,9},{2,10},{3,11},{4,12},{5,13},{6,14},{7,15},{8,0},{9,1},... | collective-permute-start | bytes 3244040 | tf_op jit(solution)/shard_map/ppermute | solution.py:270
  93.3 27.6 %pairs_last.1 = (f32[264,1024]{1,0:T(8,128)}, f32[264,1024]{1,0:T(8,128)}, f32[264,1024]{1,0:T(8,128)}, f32[264,1024]{1,0:T(8,128)}, f32[1,1024]{1,0:T(1,128)}, /*index=5*/f32[8,136,1024]{2,1,0:T(8,128)}) custom-call(s32[4]{0:T(128)} %get-tuple-element.50.refs_0_, f32[2]{0:T(128)} %pad_maximum_fusion.9.refs_1_, ...), custom_call_target="tpu_custom_call" | custom-call | flops 12884901888 | bytes 25165824 | tf_op jit(solution)/shard_map/pairs_last/pallas_call | solution.py:243
  121.6 2.9 %collective-permute-start.12 = (f32[264,1024]{1,0:T(8,128)}, f32[264,1024]{1,0:T(8,128)S(1)}, u32[]{:S(2)}, u32[]{:S(2)}) collective-permute-start(f32[264,1024]{1,0:T(8,128)} %get-tuple-element.40), channel_id=1, source_target_pairs={{0,12},{1,13},{2,14},{3,15},{4,0},{5,1},{6,2},{7,3},{8,4},{9,5},{1... | collective-permute-start | bytes 3244040 | tf_op jit(solution)/shard_map/ppermute | solution.py:270
  125.9 1.7 add_add_fusion.1
  128.6 20.5 %collective-permute-done.12 = f32[264,1024]{1,0:T(8,128)S(1)} collective-permute-done((f32[264,1024]{1,0:T(8,128)}, f32[264,1024]{1,0:T(8,128)S(1)}, u32[]{:S(2)}, u32[]{:S(2)}) %collective-permute-start.12) | collective-permute-done | bytes 1081376 | tf_op jit(solution)/shard_map/ppermute | solution.py:270
  149.1 3.7 %collective-permute-done.14 = f32[264,1024]{1,0:T(8,128)S(1)} collective-permute-done((f32[264,1024]{1,0:T(8,128)}, f32[264,1024]{1,0:T(8,128)S(1)}, u32[]{:S(2)}, u32[]{:S(2)}) %collective-permute-start.14) | collective-permute-done | bytes 1081376 | tf_op jit(solution)/shard_map/ppermute | solution.py:270
  154.4 2.5 %collective-permute-start.15 = (f32[72,2048]{1,0:T(8,128)S(1)}, f32[72,2048]{1,0:T(8,128)}, u32[]{:S(2)}, u32[]{:S(2)}) collective-permute-start(f32[72,2048]{1,0:T(8,128)S(1)} %get-tuple-element.68), channel_id=1, source_target_pairs={{0,3},{1,0},{2,1},{3,2},{4,7},{5,4},{6,5},{7,6},{8,11},{9,8},{10,9... | collective-permute-start | bytes 1769480 | tf_op jit(solution)/shard_map/ppermute | solution.py:270
  156.9 3.6 %collective-permute-start.16 = (f32[72,2048]{1,0:T(8,128)S(1)}, f32[72,2048]{1,0:T(8,128)}, u32[]{:S(2)}, u32[]{:S(2)}) collective-permute-start(f32[72,2048]{1,0:T(8,128)S(1)} %get-tuple-element.69), channel_id=1, source_target_pairs={{0,2},{1,3},{2,0},{3,1},{4,6},{5,7},{6,4},{7,5},{8,10},{9,11},{10,... | collective-permute-start | bytes 1769480 | tf_op jit(solution)/shard_map/ppermute | solution.py:270
  160.9 5.5 %collective-permute-done.15 = f32[72,2048]{1,0:T(8,128)} collective-permute-done((f32[72,2048]{1,0:T(8,128)S(1)}, f32[72,2048]{1,0:T(8,128)}, u32[]{:S(2)}, u32[]{:S(2)}) %collective-permute-start.15) | collective-permute-done | bytes 589856 | tf_op jit(solution)/shard_map/ppermute | solution.py:270
  166.4 2.2 %collective-permute-done.16 = f32[72,2048]{1,0:T(8,128)} collective-permute-done((f32[72,2048]{1,0:T(8,128)S(1)}, f32[72,2048]{1,0:T(8,128)}, u32[]{:S(2)}, u32[]{:S(2)}) %collective-permute-start.16) | collective-permute-done | bytes 589856 | tf_op jit(solution)/shard_map/ppermute | solution.py:270
  168.6 6.2 %collective-permute-done.17 = f32[72,2048]{1,0:T(8,128)} collective-permute-done((f32[72,2048]{1,0:T(8,128)S(1)}, f32[72,2048]{1,0:T(8,128)}, u32[]{:S(2)}, u32[]{:S(2)}) %collective-permute-start.17) | collective-permute-done | bytes 589856 | tf_op jit(solution)/shard_map/ppermute | solution.py:270
  174.8 1.6 fusion.3
  (76 shorter events, 17.9 us)
Async XLA Ops:
  7.2 41.4 %all-gather.2.cloned.1.call-start = ((), (), s32[]{:S(2)}) async-start(), calls=%async_computation.1 | async-start | bytes 4718592 | tf_op jit(solution)/shard_map/all_gather | solution.py:293
  7.9 170.0 %reduce-scatter.2.cloned.1.call-start = ((), (), s32[]{:S(2)}) async-start(), calls=%async_computation.2 | async-start | bytes 5013504 | tf_op jit(solution)/shard_map/reduce_scatter | solution.py:321
  7.9 10.7 %collective-permute-start = (f32[64,2048]{1,0:T(8,128)}, f32[64,2048]{1,0:T(8,128)S(1)}, u32[]{:S(2)}, u32[]{:S(2)}) collective-permute-start(f32[64,2048]{1,0:T(8,128)} %bitcast.24), channel_id=1, source_target_pairs={{0,1},{1,2},{2,3},{3,0},{4,5},{5,6},{6,7},{7,4},{8,9},{9,10},{10,1... | collective-permute-start | bytes 1572872 | tf_op jit(solution)/shard_map/ppermute | solution.py:270
  9.6 15.7 %collective-permute-start.1 = (f32[64,2048]{1,0:T(8,128)}, f32[64,2048]{1,0:T(8,128)S(1)}, u32[]{:S(2)}, u32[]{:S(2)}) collective-permute-start(f32[64,2048]{1,0:T(8,128)} %bitcast.25), channel_id=1, source_target_pairs={{0,2},{1,3},{2,0},{3,1},{4,6},{5,7},{6,4},{7,5},{8,10},{9,11},{10,... | collective-permute-start | bytes 1572872 | tf_op jit(solution)/shard_map/ppermute | solution.py:270
  12.3 13.0 %collective-permute-start.2 = (f32[64,2048]{1,0:T(8,128)}, f32[64,2048]{1,0:T(8,128)S(1)}, u32[]{:S(2)}, u32[]{:S(2)}) collective-permute-start(f32[64,2048]{1,0:T(8,128)} %bitcast.26), channel_id=1, source_target_pairs={{0,3},{1,0},{2,1},{3,2},{4,7},{5,4},{6,5},{7,6},{8,11},{9,8},{10,9... | collective-permute-start | bytes 1572872 | tf_op jit(solution)/shard_map/ppermute | solution.py:270
  25.5 10.6 %copy-start.5 = (f32[256,1024]{1,0:T(8,128)}, f32[256,1024]{1,0:T(8,128)S(1)}, u32[]{:S(2)}) copy-start(f32[256,1024]{1,0:T(8,128)S(1)} %pad_maximum_fusion.6.refs_2_) | copy-start | bytes 3145732
  25.5 33.1 %collective-permute-start.3 = (f32[256,1024]{1,0:T(8,128)S(1)}, f32[256,1024]{1,0:T(8,128)S(1)}, u32[]{:S(2)}, u32[]{:S(2)}) collective-permute-start(f32[256,1024]{1,0:T(8,128)S(1)} %pad_maximum_fusion.6.refs_2_), channel_id=1, source_target_pairs={{0,4},{1,5},{2,6},{3,7},{4,8},{5,9},{6,10},{7,11},{8,12},{9,13},{1... | collective-permute-start | bytes 3145736 | tf_op jit(solution)/shard_map/ppermute | solution.py:270
  27.1 33.2 %collective-permute-start.4 = (f32[256,1024]{1,0:T(8,128)S(1)}, f32[256,1024]{1,0:T(8,128)}, u32[]{:S(2)}, u32[]{:S(2)}) collective-permute-start(f32[256,1024]{1,0:T(8,128)S(1)} %pad_maximum_fusion.6.refs_2_), channel_id=1, source_target_pairs={{0,8},{1,9},{2,10},{3,11},{4,12},{5,13},{6,14},{7,15},{8,0},{9,1},... | collective-permute-start | bytes 3145736 | tf_op jit(solution)/shard_map/ppermute | solution.py:270
  30.0 30.3 %collective-permute-start.5 = (f32[256,1024]{1,0:T(8,128)S(1)}, f32[256,1024]{1,0:T(8,128)}, u32[]{:S(2)}, u32[]{:S(2)}) collective-permute-start(f32[256,1024]{1,0:T(8,128)S(1)} %pad_maximum_fusion.6.refs_2_), channel_id=1, source_target_pairs={{0,12},{1,13},{2,14},{3,15},{4,0},{5,1},{6,2},{7,3},{8,4},{9,5},{1... | collective-permute-start | bytes 3145736 | tf_op jit(solution)/shard_map/ppermute | solution.py:270
  36.1 55.8 %collective-permute-start.10 = (f32[256,1024]{1,0:T(8,128)}, f32[256,1024]{1,0:T(8,128)}, u32[]{:S(2)}, u32[]{:S(2)}) collective-permute-start(f32[256,1024]{1,0:T(8,128)} %pad_maximum_fusion.7.refs_6_.refs_2_), channel_id=1, source_target_pairs={{0,8},{1,9},{2,10},{3,11},{4,12},{5,13},{6,14},{7,15},{8,0},{9,1},... | collective-permute-start | bytes 3145736 | tf_op jit(solution)/shard_map/ppermute | solution.py:270
  36.4 55.9 %collective-permute-start.11 = (f32[256,1024]{1,0:T(8,128)}, f32[256,1024]{1,0:T(8,128)}, u32[]{:S(2)}, u32[]{:S(2)}) collective-permute-start(f32[256,1024]{1,0:T(8,128)} %pad_maximum_fusion.7.refs_6_.refs_2_), channel_id=1, source_target_pairs={{0,12},{1,13},{2,14},{3,15},{4,0},{5,1},{6,2},{7,3},{8,4},{9,5},{1... | collective-permute-start | bytes 3145736 | tf_op jit(solution)/shard_map/ppermute | solution.py:270
  58.6 33.7 %collective-permute-start.9 = (f32[256,1024]{1,0:T(8,128)}, f32[256,1024]{1,0:T(8,128)S(1)}, u32[]{:S(2)}, u32[]{:S(2)}) collective-permute-start(f32[256,1024]{1,0:T(8,128)} %pad_maximum_fusion.7.refs_6_.refs_2_), channel_id=1, source_target_pairs={{0,4},{1,5},{2,6},{3,7},{4,8},{5,9},{6,10},{7,11},{8,12},{9,13},{1... | collective-permute-start | bytes 3145736 | tf_op jit(solution)/shard_map/ppermute | solution.py:270
  88.9 32.0 %collective-permute-start.6 = (f32[264,1024]{1,0:T(8,128)}, f32[264,1024]{1,0:T(8,128)S(1)}, u32[]{:S(2)}, u32[]{:S(2)}) collective-permute-start(f32[264,1024]{1,0:T(8,128)} %get-tuple-element.31), channel_id=1, source_target_pairs={{0,12},{1,13},{2,14},{3,15},{4,0},{5,1},{6,2},{7,3},{8,4},{9,5},{1... | collective-permute-start | bytes 3244040 | tf_op jit(solution)/shard_map/ppermute | solution.py:270
  89.0 32.0 %collective-permute-start.7 = (f32[264,1024]{1,0:T(8,128)}, f32[264,1024]{1,0:T(8,128)S(1)}, u32[]{:S(2)}, u32[]{:S(2)}) collective-permute-start(f32[264,1024]{1,0:T(8,128)} %get-tuple-element.32), channel_id=1, source_target_pairs={{0,8},{1,9},{2,10},{3,11},{4,12},{5,13},{6,14},{7,15},{8,0},{9,1},... | collective-permute-start | bytes 3244040 | tf_op jit(solution)/shard_map/ppermute | solution.py:270
  91.9 29.0 %collective-permute-start.8 = (f32[264,1024]{1,0:T(8,128)}, f32[264,1024]{1,0:T(8,128)S(1)}, u32[]{:S(2)}, u32[]{:S(2)}) collective-permute-start(f32[264,1024]{1,0:T(8,128)} %get-tuple-element.33), channel_id=1, source_target_pairs={{0,4},{1,5},{2,6},{3,7},{4,8},{5,9},{6,10},{7,11},{8,12},{9,13},{1... | collective-permute-start | bytes 3244040 | tf_op jit(solution)/shard_map/ppermute | solution.py:270
  121.6 27.5 %collective-permute-start.12 = (f32[264,1024]{1,0:T(8,128)}, f32[264,1024]{1,0:T(8,128)S(1)}, u32[]{:S(2)}, u32[]{:S(2)}) collective-permute-start(f32[264,1024]{1,0:T(8,128)} %get-tuple-element.40), channel_id=1, source_target_pairs={{0,12},{1,13},{2,14},{3,15},{4,0},{5,1},{6,2},{7,3},{8,4},{9,5},{1... | collective-permute-start | bytes 3244040 | tf_op jit(solution)/shard_map/ppermute | solution.py:270
  124.5 24.6 %collective-permute-start.13 = (f32[264,1024]{1,0:T(8,128)}, f32[264,1024]{1,0:T(8,128)S(1)}, u32[]{:S(2)}, u32[]{:S(2)}) collective-permute-start(f32[264,1024]{1,0:T(8,128)} %get-tuple-element.41), channel_id=1, source_target_pairs={{0,8},{1,9},{2,10},{3,11},{4,12},{5,13},{6,14},{7,15},{8,0},{9,1},... | collective-permute-start | bytes 3244040 | tf_op jit(solution)/shard_map/ppermute | solution.py:270
  124.6 28.2 %collective-permute-start.14 = (f32[264,1024]{1,0:T(8,128)}, f32[264,1024]{1,0:T(8,128)S(1)}, u32[]{:S(2)}, u32[]{:S(2)}) collective-permute-start(f32[264,1024]{1,0:T(8,128)} %get-tuple-element.42), channel_id=1, source_target_pairs={{0,4},{1,5},{2,6},{3,7},{4,8},{5,9},{6,10},{7,11},{8,12},{9,13},{1... | collective-permute-start | bytes 3244040 | tf_op jit(solution)/shard_map/ppermute | solution.py:270
  127.6 25.1 %copy-start.4 = (f32[264,1024]{1,0:T(8,128)S(1)}, f32[264,1024]{1,0:T(8,128)}, u32[]{:S(2)}) copy-start(f32[264,1024]{1,0:T(8,128)} %get-tuple-element.35) | copy-start | bytes 3244036
  154.3 6.3 %slice-start.1 = ((f32[264,1024]{1,0:T(8,128)}), f32[72,1024]{1,0:T(8,128)S(1)}, s32[]{:S(2)}) async-start(f32[264,1024]{1,0:T(8,128)} %copy-done.1), calls=%async_computation.4 | async-start | bytes 589824 | tf_op jit(solution)/shard_map/concatenate | solution.py:324
  154.4 6.3 %copy-start.2 = (f32[1024,128]{1,0:T(8,128)S(1)}, f32[1024,128]{1,0:T(8,128)}, u32[]{:S(2)}) copy-start(f32[1024,128]{1,0:T(8,128)} %param.5) | copy-start | bytes 1572868
  154.4 12.0 %collective-permute-start.15 = (f32[72,2048]{1,0:T(8,128)S(1)}, f32[72,2048]{1,0:T(8,128)}, u32[]{:S(2)}, u32[]{:S(2)}) collective-permute-start(f32[72,2048]{1,0:T(8,128)S(1)} %get-tuple-element.68), channel_id=1, source_target_pairs={{0,3},{1,0},{2,1},{3,2},{4,7},{5,4},{6,5},{7,6},{8,11},{9,8},{10,9... | collective-permute-start | bytes 1769480 | tf_op jit(solution)/shard_map/ppermute | solution.py:270
  156.9 11.7 %collective-permute-start.16 = (f32[72,2048]{1,0:T(8,128)S(1)}, f32[72,2048]{1,0:T(8,128)}, u32[]{:S(2)}, u32[]{:S(2)}) collective-permute-start(f32[72,2048]{1,0:T(8,128)S(1)} %get-tuple-element.69), channel_id=1, source_target_pairs={{0,2},{1,3},{2,0},{3,1},{4,6},{5,7},{6,4},{7,5},{8,10},{9,11},{10,... | collective-permute-start | bytes 1769480 | tf_op jit(solution)/shard_map/ppermute | solution.py:270
  160.6 14.2 %collective-permute-start.17 = (f32[72,2048]{1,0:T(8,128)S(1)}, f32[72,2048]{1,0:T(8,128)}, u32[]{:S(2)}, u32[]{:S(2)}) collective-permute-start(f32[72,2048]{1,0:T(8,128)S(1)} %pad_maximum_fusion.8), channel_id=1, source_target_pairs={{0,1},{1,2},{2,3},{3,0},{4,5},{5,6},{6,7},{7,4},{8,9},{9,10},{10,1... | collective-permute-start | bytes 1769480 | tf_op jit(solution)/shard_map/ppermute | solution.py:270
  (9 other events, 22.7 us)
Sparse Core Ops, SparseCore 0:
  9.7 38.8 all-gather.1
  121.7 44.5 reduce-scatter.1
